TPU v7x, 128 devices: a whole 4x4x4 slice. The times are simulated.
128 devices in a mesh: frames: 64 (over z, y, x_lo, core), dp: 2 (over x_hi).
Axes of the slice: x: 4 (x_hi: 2, x_lo: 2; x = x_hi * 2 + x_lo), y: 4, z: 4, core: 2. Of those that a mesh axis runs over, the one named last changes fastest.
Arguments:
- shifted: bfloat16 [2, 256, 16, 16, 640], P('dp', 'frames'), may hold values from -6 to 6
- out_grad: bfloat16 [2, 256, 16, 16, 640], P('dp', 'frames'), may hold values from -6 to 6
- conv_weight: bfloat16 [640, 5760], P('frames'), may hold values from -0.078125 to 0.078125
- norm_gain: float32 [640], replicated, may hold values from 0.5 to 2
- norm_bias: float32 [640], replicated, may hold values from -4 to 4
- shift_fwd: int32 [80], replicated, may hold values from 0 to 639, as said below
- shift_bwd: int32 [80], replicated, may hold values from 0 to 639, as said below
Outputs:
- in_grad: bfloat16 [2, 256, 16, 16, 640], P('dp', 'frames')
- weight_grad: float32 [640, 5760], P('frames')
- gain_grad: float32 [640], replicated
- bias_grad: float32 [640], replicated
Inputs may be any that keep to these rules, and one draw needn't show every extreme that they name: `shift_fwd`: 80 distinct channel numbers, none of them in shift_bwd. `shift_bwd`: 80 distinct channel numbers, none of them in shift_fwd.
All inputs are finite; a program needn't handle non-finite values.
Results may differ from a plain program's by a relative error of at most 0.003.
Values may be sent and summed in bfloat16 or wider, within the bound.
A program may use at most 128 MiB of HBM per device.

v0:
```python
import jax
import jax.numpy as jnp
from jax import lax
from jax.sharding import PartitionSpec as P

GROUP_CH = 20
epsilon = 1e-05


def with_halo(x, sides, width):
    for axis, dim in sides:
        size, length = (lax.axis_size(axis), x.shape[dim])
        up = [(i, (i + 1) % size) for i in range(size - 1)]
        down = [(j, i) for i, j in up]
        last = lax.slice_in_dim(x, length - width, length, axis=dim)
        first = lax.slice_in_dim(x, 0, width, axis=dim)
        before = lax.ppermute(last, axis, up)
        after = lax.ppermute(first, axis, down)
        x = jnp.concatenate([before, x, after], axis=dim)
    return x


def pad_space(values):
    return jnp.pad(values, ((0, 0), (1, 1), (1, 1), (0, 0)))


def on_device(shifted, out_grad, conv_weight, norm_gain, norm_bias, shift_fwd, shift_bwd):
    frames_local = shifted[0]
    grad_local = out_grad[0]
    frame_count, row_count, col_count, channels = frames_local.shape
    groups = channels // GROUP_CH
    whole_weight = lax.all_gather(conv_weight, "frames", axis=0, tiled=True)
    values = frames_local.astype(jnp.float32).reshape(
        frame_count, row_count * col_count, groups, GROUP_CH
    )
    center = jnp.mean(values, axis=(1, 3), keepdims=True)
    spread = jnp.mean(jnp.square(values - center), axis=(1, 3), keepdims=True)
    inverse = lax.rsqrt(spread + epsilon)
    grouped_normed = (values - center) * inverse
    normed = grouped_normed.reshape(frame_count, row_count, col_count, channels)
    before = normed * norm_gain + norm_bias
    activation = jax.nn.silu(before).astype(jnp.bfloat16)
    act_padded = pad_space(activation)
    grad_padded = pad_space(grad_local)
    grad_rows = grad_local.reshape(-1, channels)
    act_grad = jnp.zeros((grad_rows.shape[0], channels), jnp.float32)
    for tap_index in range(9):
        row_off, col_off = divmod(tap_index, 3)
        grad_view = grad_padded[
            :, 2 - row_off : 2 - row_off + row_count, 2 - col_off : 2 - col_off + col_count, :
        ].reshape(-1, channels)
        act_grad = act_grad + jnp.dot(
            grad_view,
            whole_weight[:, tap_index * channels : (tap_index + 1) * channels],
            preferred_element_type=jnp.float32,
        )
    scale = float(
        lax.axis_size("dp") * lax.axis_size("frames") * frame_count * row_count * col_count
    ) ** (-0.5)
    parts = []
    for tap_index in range(9):
        row_off, col_off = divmod(tap_index, 3)
        act_view = act_padded[
            :, row_off : row_off + row_count, col_off : col_off + col_count, :
        ].reshape(-1, channels)
        parts.append(
            lax.dot_general(
                grad_rows, act_view, (((0,), (0,)), ((), ())), preferred_element_type=jnp.float32
            )
        )
    kernel_shard = lax.psum_scatter(
        jnp.concatenate(parts, axis=1), "frames", scatter_dimension=0, tiled=True
    )
    kernel_shard = lax.psum(kernel_shard, "dp")
    weight_grad = kernel_shard * scale
    sigmoid_val = jax.nn.sigmoid(before)
    pre_grad = act_grad.reshape(before.shape) * sigmoid_val * (1.0 + before * (1.0 - sigmoid_val))
    gain_part = jnp.sum(pre_grad * normed, axis=(0, 1, 2))
    bias_part = jnp.sum(pre_grad, axis=(0, 1, 2))
    gain_total, bias_total = lax.psum((gain_part, bias_part), ("frames", "dp"))
    norm_grad = (pre_grad * norm_gain).reshape(values.shape)
    first_mean = jnp.mean(norm_grad, axis=(1, 3), keepdims=True)
    second_mean = jnp.mean(norm_grad * grouped_normed, axis=(1, 3), keepdims=True)
    shifted_grad = (
        ((norm_grad - first_mean - grouped_normed * second_mean) * inverse)
        .reshape(frames_local.shape)
        .astype(jnp.bfloat16)
    )
    channel_ids = jnp.arange(channels, dtype=jnp.int32)
    forward_match = channel_ids[None, :] == shift_fwd[:, None]
    backward_match = channel_ids[None, :] == shift_bwd[:, None]
    forward_select = forward_match.astype(jnp.bfloat16)
    backward_select = backward_match.astype(jnp.bfloat16)
    forward_mask = jnp.any(forward_match, axis=0)
    backward_mask = jnp.any(backward_match, axis=0)
    plane = row_count * col_count
    first_frame = shifted_grad[0].reshape(plane, channels)
    last_frame = shifted_grad[frame_count - 1].reshape(plane, channels)
    contract_channels = (((1,), (1,)), ((), ()))
    rim_first = lax.dot_general(
        forward_select, first_frame, contract_channels, preferred_element_type=jnp.float32
    ).astype(jnp.bfloat16)
    rim_last = lax.dot_general(
        backward_select, last_frame, contract_channels, preferred_element_type=jnp.float32
    ).astype(jnp.bfloat16)
    extended = with_halo(jnp.stack([rim_first, rim_last]), (("frames", 0),), 1)
    contract_fold = (((0,), (0,)), ((), ()))
    from_prev = lax.dot_general(
        extended[0], backward_select, contract_fold, preferred_element_type=jnp.float32
    ).astype(jnp.bfloat16)
    from_next = lax.dot_general(
        extended[3], forward_select, contract_fold, preferred_element_type=jnp.float32
    ).astype(jnp.bfloat16)
    from_prev = from_prev.reshape(1, row_count, col_count, channels)
    from_next = from_next.reshape(1, row_count, col_count, channels)
    later = jnp.concatenate([shifted_grad[1:], from_next], axis=0)
    earlier = jnp.concatenate([from_prev, shifted_grad[:-1]], axis=0)
    in_grad = jnp.where(forward_mask, later, jnp.where(backward_mask, earlier, shifted_grad))
    return (in_grad[None], weight_grad, gain_total * scale, bias_total * scale)


def solution(mesh):
    in_specs = (
        P("dp", "frames", None, None, None),
        P("dp", "frames", None, None, None),
        P("frames", None),
        P(),
        P(),
        P(),
        P(),
    )
    out_specs = (P("dp", "frames", None, None, None), P("frames", None), P(), P())
    return jax.shard_map(
        on_device, mesh=mesh, in_specs=in_specs, out_specs=out_specs, check_vma=False
    )
```

profile of v0, /device:TPU:1, one launch (start us, length us, event | category | flops | bytes accessed | tf_op | source)
XLA Modules:
  0.0 923.6 jit_solution(15676079137542957894)
XLA Ops:
  7.2 0.7 all-gather.3.cloned.1.call-update
  8.0 21.9 %reshape.226 = f32[4,256,32,20]{3,2,1,0:T(8,128)} reshape(bf16[1,4,16,16,640]{4,3,2,1,0:T(8,128)(2,1)} %param.7) | data formatting | bytes 3932160 | tf_op jit(solution)/shard_map/convert_element_type | solution.py:33
  30.6 0.4 multiply_reduce_fusion.2
  31.5 11.5 %copy.33 = f32[4,256,32,20]{1,0,3,2:T(4,128)} copy(f32[4,256,32,20]{3,2,1,0:T(8,128)} %reshape.226) | data formatting | bytes 5242880 | tf_op jit(solution)/shard_map/convert_element_type | solution.py:33
  43.2 8.8 pad_slice_fusion.8
  52.0 78.7 %all-gather.3.cloned.1.call-done = bf16[64,10,5760]{2,1,0:T(8,128)(2,1)} async-done(((bf16[1,10,5760]{2,1,0:T(8,128)(2,1)}), bf16[64,10,5760]{2,1,0:T(8,128)(2,1)}) %all-gather.3.cloned.1.call-update) | async-done | bytes 7372816 | tf_op jit(solution)/shard_map/all_gather | solution.py:32
  130.7 13.8 %reshape.229 = bf16[640,5760]{1,0:T(8,128)(2,1)} reshape(bf16[64,10,5760]{2,1,0:T(8,128)(2,1)} %all-gather.3.cloned.1.call-done) | data formatting | bytes 14745600
  144.6 3.0 fusion.4
  147.6 0.7 copy-done.1
  148.3 0.3 copy-done.11
  148.6 1.3 fusion.6
  149.9 1.3 fusion.8
  151.3 1.3 fusion.10
  152.6 1.3 fusion.12
  154.0 1.3 fusion.14
  155.3 2.8 fusion.18
  158.1 2.8 fusion.16
  160.9 6.2 fusion.28
  167.1 3.3 copy.31
  170.3 4.2 reshape.215
  174.5 16.5 %fusion.29 = (f32[4,32]{0,1:T(8,128)S(1)}, f32[4,32]{0,1:T(8,128)S(1)}) fusion(f32[4,32]{0,1:T(8,128)S(1)} %copy.34, f32[4,256,32,20]{1,0,3,2:T(4,128)} %copy.33, f32[4,32]{0,1:T(8,128)S(1)} %copy.32, f32[4,256,32,20]{1,0,3,2:T(4,128)} %reshape.215, f32[32,20]{1,0:T(8,128)S(1)} %add.134, f32[32,20]{1,0:T(8,128)S(1)} %mul.201), kind=kLoop, calls=%fused_computation.88 | loop fusion | flops 10485504 | bytes 5250048 | tf_op jit(solution)/shard_map/reduce_sum | solution.py:82
  191.6 3.6 multiply_convert_fusion
  195.2 3.0 pad_slice_fusion
  198.2 2.4 bitcast_dynamic-update-slice_fusion.8
  200.6 2.4 bitcast_dynamic-update-slice_fusion.7
  203.0 2.4 bitcast_dynamic-update-slice_fusion.6
  205.5 2.4 bitcast_dynamic-update-slice_fusion.5
  207.9 2.4 bitcast_dynamic-update-slice_fusion.4
  210.3 2.4 bitcast_dynamic-update-slice_fusion.3
  212.7 2.5 bitcast_dynamic-update-slice_fusion.2
  215.2 2.4 bitcast_dynamic-update-slice_fusion.1
  217.6 2.4 bitcast_dynamic-update-slice_fusion
  220.1 0.6 copy-done.16
  220.7 0.6 dynamic-slice
  222.4 2.2 collective-permute-start
  224.9 3.4 collective-permute-start.1
  228.2 67.9 %all-reduce.3 = (f32[640]{0:T(1024)S(1)}, f32[640]{0:T(1024)S(1)}) all-reduce(f32[640]{0:T(1024)S(1)} %get-tuple-element.25, f32[640]{0:T(1024)S(1)} %get-tuple-element.24), channel_id=1, replica_groups=mesh['frames'=64,'dp'=2] {'frames','dp'}, use_global_device_ids=true, to_apply=%region_11.12 | all-reduce | flops 1280 | bytes 10240 | tf_op jit(solution)/shard_map/psum | solution.py:80
  296.1 1.5 slice_bitcast_fusion
  297.6 0.6 broadcast_multiply_fusion.1
  298.2 1.0 convolution_convert_fusion.1
  299.2 1.0 convolution_convert_fusion
  300.3 516.5 %all-reduce.9.cloned.1.call-done = f32[640,5760]{0,1:T(8,128)} async-done(((f32[640,5760]{0,1:T(8,128)}), f32[640,5760]{0,1:T(8,128)}) %all-reduce.9.cloned.1.call-update) | async-done | bytes 14745616
  816.7 5.1 constant_dynamic-slice_fusion
  821.8 1.2 copy-done.2
  823.3 4.4 maximum_select_fusion
  827.7 82.4 %all-reduce.7.cloned.1.call-done = f32[10,5760]{0,1:T(8,128)} async-done(((f32[10,5760]{0,1:T(8,128)}), f32[10,5760]{0,1:T(8,128)}) %all-reduce.7.cloned.1.call-update) | async-done | bytes 230416 | tf_op jit(solution)/shard_map/psum | solution.py:74
  910.1 3.7 broadcast_multiply_fusion
  913.8 3.0 copy.37
  (64 shorter events, 3.1 us)
Async XLA Ops:
  7.2 123.5 %all-gather.3.cloned.1.call-start = ((), (), s32[]{:S(2)}) async-start(), calls=%async_computation.1 | async-start | bytes 11980800 | tf_op jit(solution)/shard_map/all_gather | solution.py:32
  7.9 22.0 %copy-start = (bf16[1,4,16,16,640]{4,3,2,1,0:T(8,128)(2,1)S(1)}, bf16[1,4,16,16,640]{4,3,2,1,0:T(8,128)(2,1)}, u32[]{:S(2)}) copy-start(bf16[1,4,16,16,640]{4,3,2,1,0:T(8,128)(2,1)} %param.7) | copy-start | bytes 3932164
  7.9 808.8 %all-reduce.9.cloned.1.call-start = ((), (), s32[]{:S(2)}) async-start(), calls=%async_computation.2 | async-start | bytes 29491200
  31.5 11.5 %copy-start.12 = (f32[640]{0:T(1024)S(1)}, f32[640]{0:T(1024)}, u32[]{:S(2)}) copy-start(f32[640]{0:T(1024)} %param.11) | copy-start | bytes 7684
  31.5 11.6 %copy-start.13 = (f32[640]{0:T(1024)S(1)}, f32[640]{0:T(1024)}, u32[]{:S(2)}) copy-start(f32[640]{0:T(1024)} %param.10) | copy-start | bytes 7684
  144.5 3.7 copy-start.1
  144.6 4.0 copy-start.11
  148.6 1.3 copy-start.10
  149.9 1.3 copy-start.4
  151.3 1.3 copy-start.9
  152.6 1.3 copy-start.8
  154.0 1.3 copy-start.7
  155.3 2.8 copy-start.6
  195.2 3.0 copy-start.5
  220.1 0.7 copy-start.16
  220.1 1.9 copy-start.14
  220.1 1.9 copy-start.15
  220.1 690.0 %all-reduce.7.cloned.1.call-start = ((), (), s32[]{:S(2)}) async-start(), calls=%async_computation | async-start | bytes 5898240 | tf_op jit(solution)/shard_map/psum | solution.py:74
  222.4 75.8 %collective-permute-start = (bf16[1,80,256]{2,1,0:T(8,128)(2,1)S(1)}, bf16[1,80,256]{2,1,0:T(8,128)(2,1)S(1)}, u32[]{:S(2)}, u32[]{:S(2)}) collective-permute-start(bf16[1,80,256]{2,1,0:T(8,128)(2,1)S(1)} %fusion.1), channel_id=1, source_target_pairs={{2,0},{4,2},{6,4},{8,6},{10,8},{12,10},{14,12},{16,14},{18,16},{20... | collective-permute-start | bytes 122888 | tf_op jit(solution)/shard_map/ppermute | solution.py:18
  224.9 74.4 %collective-permute-start.1 = (bf16[1,80,256]{2,1,0:T(8,128)(2,1)S(1)}, bf16[1,80,256]{2,1,0:T(8,128)(2,1)S(1)}, u32[]{:S(2)}, u32[]{:S(2)}) collective-permute-start(bf16[1,80,256]{2,1,0:T(8,128)(2,1)S(1)} %fusion.2), channel_id=1, source_target_pairs={{0,2},{2,4},{4,6},{6,8},{8,10},{10,12},{12,14},{14,16},{16,18},{18... | collective-permute-start | bytes 122888 | tf_op jit(solution)/shard_map/ppermute | solution.py:17
  821.8 1.2 copy-start.2
  821.8 1.5 copy-start.3
Sparse Core Ops, SparseCore 0:
  9.7 120.9 all-gather.2
  220.2 596.4 all-reduce.8
  822.0 88.0 all-reduce.6
where the time goes:
time: 929 us; the launch traced here: 924 us
  waiting for transfers between devices  678 us (73%)
  local copies, waits for them, and re-layouts  81.4 us (9%)
  blocking collectives  67.9 us (7%)
  matrix products  45.7 us (5%)
  other arithmetic  29.7 us (3%)
  between operations  15 us (2%)
    unnamed x4, waiting for transfers between devices  517 us
    psum x1, waiting for transfers between devices, on_device(): kernel_shard = lax.psum(kernel_shard, 'dp')  82.4 us
    all_gather x1, waiting for transfers between devices, on_device(): whole_weight = lax.all_gather(conv_weight, 'frames', axis=0, tiled=True)  78.7 us
    psum x1, blocking collectives, on_device(): gain_total, bias_total = lax.psum((gain_part, bias_part), ('frames', 'dp'))  67.9 us
    convert_element_type x2, local copies, waits for them, and re-layouts, on_device(): frames_local.astype(jnp.float32)  33.4 us
    unnamed x38, local copies, waits for them, and re-layouts  25.6 us
    dot_general x9, matrix products, on_device(): lax.dot_general(grad_rows, act_view, (((0,), (0,)), ((), ())), preferred_...  21.8 us
    dot_general x9, matrix products, on_device(): jnp.dot(grad_view, whole_weight[:, tap_index * channels:(tap_index + 1) *...  21.3 us
  transfers between devices with their start and end apart: 5, of which 3 were waited for; matrix products, arithmetic and copies ran while one was open for 6% of the time, Pallas kernels for 0%

commit v1 on v0

--- a/solution.py
+++ b/solution.py
@@ -29,7 +29,10 @@
     grad_local = out_grad[0]
     frame_count, row_count, col_count, channels = frames_local.shape
     groups = channels // GROUP_CH
-    whole_weight = lax.all_gather(conv_weight, "frames", axis=0, tiled=True)
+    count = lax.axis_size("frames")
+    blocks = jnp.stack([conv_weight for _ in range(count)])
+    blocks = lax.all_to_all(blocks, "frames", split_axis=0, concat_axis=0)
+    whole_weight = jnp.concatenate(blocks, axis=0)
     values = frames_local.astype(jnp.float32).reshape(
         frame_count, row_count * col_count, groups, GROUP_CH
     )

time: 929 us -> 999 us (1.075)
  starting transfers between devices: 5.68 us -> 37.5 us
  waiting for transfers between devices: 678 us -> 709 us
    all_to_all x0 -> x1, waiting for transfers between devices: none -> 109 us  [on_device(): blocks = lax.all_to_all(blocks, 'frames', split_axis=0, concat_axis=0)]
    all_gather x1 -> x0, waiting for transfers between devices: 78.7 us -> none  [on_device(): whole_weight = lax.all_gather(conv_weight, 'frames', axis=0, tiled=True)]
    ppermute x1, starting transfers between devices: 3.38 us -> 23.5 us  [with_halo(): before = lax.ppermute(last, axis, up)]
    reshape x0 -> x1, local copies, waits for them, and re-layouts: none -> 13.8 us  [on_device(): whole_weight = jnp.concatenate(blocks, axis=0)]
    unnamed x38 -> x37, local copies, waits for them, and re-layouts: 25.6 us -> 11.8 us
    all_to_all x0 -> x1, starting transfers between devices: none -> 11.2 us  [on_device(): blocks = lax.all_to_all(blocks, 'frames', split_axis=0, concat_axis=0)]
    unnamed x4 -> x3, waiting for transfers between devices: 517 us -> 518 us
  transfers between devices with their start and end apart: 5 -> 5, of which waited for: 3 -> 3; matrix products, arithmetic and copies ran while one was open for 6% -> 5% of each run, Pallas kernels for 0% -> 0%
where the time goes in v1:
time: 999 us; the launch traced here: 992 us
  waiting for transfers between devices  709 us (71%)
  local copies, waits for them, and re-layouts  85.5 us (9%)
  blocking collectives  69.7 us (7%)
  matrix products  45.7 us (5%)
  starting transfers between devices  37.5 us (4%)
  other arithmetic  29.7 us (3%)
  between operations  15.3 us (2%)
    unnamed x3, waiting for transfers between devices  518 us
    all_to_all x1, waiting for transfers between devices, on_device(): blocks = lax.all_to_all(blocks, 'frames', split_axis=0, concat_axis=0)  109 us
    psum x1, waiting for transfers between devices, on_device(): kernel_shard = lax.psum(kernel_shard, 'dp')  82.4 us
    psum x1, blocking collectives, on_device(): gain_total, bias_total = lax.psum((gain_part, bias_part), ('frames', 'dp'))  69.7 us
    convert_element_type x2, local copies, waits for them, and re-layouts, on_device(): frames_local.astype(jnp.float32)  32 us
    ppermute x1, starting transfers between devices, with_halo(): before = lax.ppermute(last, axis, up)  23.5 us
    dot_general x9, matrix products, on_device(): lax.dot_general(grad_rows, act_view, (((0,), (0,)), ((), ())), preferred_...  21.8 us
    dot_general x9, matrix products, on_device(): jnp.dot(grad_view, whole_weight[:, tap_index * channels:(tap_index + 1) *...  21.4 us
  transfers between devices with their start and end apart: 5, of which 3 were waited for; matrix products, arithmetic and copies ran while one was open for 5% of the time, Pallas kernels for 0%

profile of v1, /device:TPU:1, one launch (start us, length us, event | category | flops | bytes accessed | tf_op | source)
XLA Modules:
  0.0 992.5 jit_solution(17211687461772730011)
XLA Ops:
  7.2 6.0 stack.6
  13.1 11.2 %all-to-all-start = ((bf16[64,10,5760]{2,1,0:T(8,128)(2,1)}), bf16[64,10,5760]{2,1,0:T(8,128)(2,1)}, u32[]{:S(2)}, u32[]{:S(2)}) async-start(bf16[64,10,5760]{2,1,0:T(8,128)(2,1)} %stack.6), calls=%async_computation | async-start | bytes 23592960 | tf_op jit(solution)/shard_map/all_to_all | solution.py:34
  24.4 20.6 %reshape.232 = f32[4,256,32,20]{3,2,1,0:T(8,128)} reshape(bf16[1,4,16,16,640]{4,3,2,1,0:T(8,128)(2,1)S(1)} %copy-done) | data formatting | bytes 3932160 | tf_op jit(solution)/shard_map/convert_element_type | solution.py:36
  45.7 0.4 multiply_reduce_fusion.2
  46.6 11.4 %copy.33 = f32[4,256,32,20]{1,0,3,2:T(4,128)} copy(f32[4,256,32,20]{3,2,1,0:T(8,128)} %reshape.232) | data formatting | bytes 5242880 | tf_op jit(solution)/shard_map/convert_element_type | solution.py:36
  58.2 8.5 pad_slice_fusion.8
  66.7 108.5 %all-to-all-done = bf16[64,10,5760]{2,1,0:T(8,128)(2,1)} async-done(((bf16[64,10,5760]{2,1,0:T(8,128)(2,1)}), bf16[64,10,5760]{2,1,0:T(8,128)(2,1)}, u32[]{:S(2)}, u32[]{:S(2)}) %all-to-all-start) | async-done | bytes 7372832 | tf_op jit(solution)/shard_map/all_to_all | solution.py:34
  175.2 13.8 %reshape.211 = bf16[640,5760]{1,0:T(8,128)(2,1)} reshape(bf16[64,10,5760]{2,1,0:T(8,128)(2,1)} %all-to-all-done) | data formatting | bytes 14745600 | tf_op jit(solution)/shard_map/reshape | solution.py:35
  189.1 3.0 fusion.4
  192.1 0.7 copy-done.1
  193.1 1.3 fusion.6
  194.5 1.3 fusion.8
  195.8 1.3 fusion.10
  197.2 1.3 fusion.12
  198.5 1.3 fusion.14
  199.8 2.8 fusion.18
  202.6 2.8 fusion.16
  205.5 6.2 fusion.28
  211.6 3.2 copy.31
  214.9 4.2 reshape.221
  219.1 16.5 %fusion.29 = (f32[4,32]{0,1:T(8,128)S(1)}, f32[4,32]{0,1:T(8,128)S(1)}) fusion(f32[4,32]{0,1:T(8,128)S(1)} %copy.34, f32[4,256,32,20]{1,0,3,2:T(4,128)} %copy.33, f32[4,32]{0,1:T(8,128)S(1)} %copy.32, f32[4,256,32,20]{1,0,3,2:T(4,128)} %reshape.221, f32[32,20]{1,0:T(8,128)S(1)} %add.134, f32[32,20]{1,0:T(8,128)S(1)} %mul.201), kind=kLoop, calls=%fused_computation.88 | loop fusion | flops 10485504 | bytes 5250048 | tf_op jit(solution)/shard_map/reduce_sum | solution.py:85
  236.1 3.6 multiply_convert_fusion
  239.7 3.0 pad_slice_fusion
  242.7 2.4 bitcast_dynamic-update-slice_fusion.8
  245.2 2.4 bitcast_dynamic-update-slice_fusion.7
  247.6 2.4 bitcast_dynamic-update-slice_fusion.6
  250.0 2.4 bitcast_dynamic-update-slice_fusion.5
  252.4 2.4 bitcast_dynamic-update-slice_fusion.4
  254.8 2.4 bitcast_dynamic-update-slice_fusion.3
  257.2 2.5 bitcast_dynamic-update-slice_fusion.2
  259.7 2.4 bitcast_dynamic-update-slice_fusion.1
  262.2 2.4 bitcast_dynamic-update-slice_fusion
  264.7 0.6 copy-done.16
  265.2 0.6 dynamic-slice
  266.9 2.7 collective-permute-start
  269.9 23.5 %collective-permute-start.1 = (bf16[1,80,256]{2,1,0:T(8,128)(2,1)S(1)}, bf16[1,80,256]{2,1,0:T(8,128)(2,1)S(1)}, u32[]{:S(2)}, u32[]{:S(2)}) collective-permute-start(bf16[1,80,256]{2,1,0:T(8,128)(2,1)S(1)} %fusion.2), channel_id=1, source_target_pairs={{0,2},{2,4},{4,6},{6,8},{8,10},{10,12},{12,14},{14,16},{16,18},{18... | collective-permute-start | bytes 122888 | tf_op jit(solution)/shard_map/ppermute | solution.py:17
  293.4 69.7 %all-reduce.3 = (f32[640]{0:T(1024)S(1)}, f32[640]{0:T(1024)S(1)}) all-reduce(f32[640]{0:T(1024)S(1)} %get-tuple-element.25, f32[640]{0:T(1024)S(1)} %get-tuple-element.24), channel_id=1, replica_groups=mesh['frames'=64,'dp'=2] {'frames','dp'}, use_global_device_ids=true, to_apply=%region_11.12 | all-reduce | flops 1280 | bytes 10240 | tf_op jit(solution)/shard_map/psum | solution.py:83
  363.1 1.4 slice_bitcast_fusion
  364.6 0.6 broadcast_multiply_fusion.1
  365.2 1.0 convolution_convert_fusion.1
  366.2 1.0 convolution_convert_fusion
  367.2 518.1 %all-reduce.9.cloned.1.call-done = f32[640,5760]{0,1:T(8,128)} async-done(((f32[640,5760]{0,1:T(8,128)}), f32[640,5760]{0,1:T(8,128)}) %all-reduce.9.cloned.1.call-update) | async-done | bytes 14745616
  885.3 5.1 constant_dynamic-slice_fusion
  890.4 1.2 copy-done.2
  891.9 4.4 maximum_select_fusion
  896.3 82.4 %all-reduce.7.cloned.1.call-done = f32[10,5760]{0,1:T(8,128)} async-done(((f32[10,5760]{0,1:T(8,128)}), f32[10,5760]{0,1:T(8,128)}) %all-reduce.7.cloned.1.call-update) | async-done | bytes 230416 | tf_op jit(solution)/shard_map/psum | solution.py:77
  978.7 3.7 broadcast_multiply_fusion
  982.4 3.0 copy.37
  (64 shorter events, 3.4 us)
Async XLA Ops:
  13.1 11.3 %copy-start = (bf16[1,4,16,16,640]{4,3,2,1,0:T(8,128)(2,1)S(1)}, bf16[1,4,16,16,640]{4,3,2,1,0:T(8,128)(2,1)}, u32[]{:S(2)}) copy-start(bf16[1,4,16,16,640]{4,3,2,1,0:T(8,128)(2,1)} %param.7) | copy-start | bytes 3932164
  13.1 162.1 %all-to-all-start = ((bf16[64,10,5760]{2,1,0:T(8,128)(2,1)}), bf16[64,10,5760]{2,1,0:T(8,128)(2,1)}, u32[]{:S(2)}, u32[]{:S(2)}) async-start(bf16[64,10,5760]{2,1,0:T(8,128)(2,1)} %stack.6), calls=%async_computation | async-start | bytes 23592960 | tf_op jit(solution)/shard_map/all_to_all | solution.py:34
  24.4 861.0 %all-reduce.9.cloned.1.call-start = ((), (), s32[]{:S(2)}) async-start(), calls=%async_computation.2 | async-start | bytes 29491200
  46.6 11.4 %copy-start.12 = (f32[640]{0:T(1024)S(1)}, f32[640]{0:T(1024)}, u32[]{:S(2)}) copy-start(f32[640]{0:T(1024)} %param.11) | copy-start | bytes 7684
  46.6 11.5 %copy-start.13 = (f32[640]{0:T(1024)S(1)}, f32[640]{0:T(1024)}, u32[]{:S(2)}) copy-start(f32[640]{0:T(1024)} %param.10) | copy-start | bytes 7684
  189.1 3.7 copy-start.1
  189.1 4.0 copy-start.11
  193.1 1.3 copy-start.10
  194.5 1.3 copy-start.4
  195.8 1.3 copy-start.9
  197.1 1.3 copy-start.8
  198.5 1.3 copy-start.7
  199.8 2.8 copy-start.6
  239.7 3.0 copy-start.5
  264.6 0.7 copy-start.16
  264.6 1.9 copy-start.14
  264.6 1.9 copy-start.15
  264.6 714.1 %all-reduce.7.cloned.1.call-start = ((), (), s32[]{:S(2)}) async-start(), calls=%async_computation.1 | async-start | bytes 5898240 | tf_op jit(solution)/shard_map/psum | solution.py:77
  266.9 98.2 %collective-permute-start = (bf16[1,80,256]{2,1,0:T(8,128)(2,1)S(1)}, bf16[1,80,256]{2,1,0:T(8,128)(2,1)S(1)}, u32[]{:S(2)}, u32[]{:S(2)}) collective-permute-start(bf16[1,80,256]{2,1,0:T(8,128)(2,1)S(1)} %fusion.1), channel_id=1, source_target_pairs={{2,0},{4,2},{6,4},{8,6},{10,8},{12,10},{14,12},{16,14},{18,16},{20... | collective-permute-start | bytes 122888 | tf_op jit(solution)/shard_map/ppermute | solution.py:18
  269.9 96.2 %collective-permute-start.1 = (bf16[1,80,256]{2,1,0:T(8,128)(2,1)S(1)}, bf16[1,80,256]{2,1,0:T(8,128)(2,1)S(1)}, u32[]{:S(2)}, u32[]{:S(2)}) collective-permute-start(bf16[1,80,256]{2,1,0:T(8,128)(2,1)S(1)} %fusion.2), channel_id=1, source_target_pairs={{0,2},{2,4},{4,6},{6,8},{8,10},{10,12},{12,14},{14,16},{16,18},{18... | collective-permute-start | bytes 122888 | tf_op jit(solution)/shard_map/ppermute | solution.py:17
  890.4 1.2 copy-start.2
  890.4 1.5 copy-start.3
Sparse Core Ops, SparseCore 0:
  264.7 620.5 all-reduce.8
  890.5 88.0 all-reduce.6
